TPU v7x, 32 devices: a whole 2x2x4 slice. The times are simulated.
32 devices in a mesh: seq: 4 (over y, x), tensor: 8 (over z, core).
Axes of the slice: x: 2, y: 2, z: 4, core: 2. Of those that a mesh axis runs over, the one named last changes fastest.
Arguments:
- tokens: bfloat16 [4096, 4096], P(('seq', 'tensor')), may hold values from -36 to 36
- norm_gain: float32 [4096], replicated, may hold values from 0.1 to 1.9
- in_weight: bfloat16 [4096, 3, 4096], P(None, None, 'tensor'), may hold values from -0.09375 to 0.09375
- short_filter: float32 [3, 3, 4096], P(None, None, 'tensor'), may hold values from -3 to 3
- filter_spectrum: float32 [2, 8, 4096, 1024], P(None, 'seq', 'tensor'), may hold values from -4 to 4
- out_weight: bfloat16 [4096, 4096], P('tensor'), may hold values from -0.09375 to 0.09375
Outputs:
- mixer_out: bfloat16 [4096, 4096], P(('seq', 'tensor'))
All inputs are finite; a program needn't handle non-finite values.
Results may differ from a plain program's by a relative error of at most 0.012.
Values may be sent and summed in bfloat16 or wider, within the bound.
A program may use at most 192 MiB of HBM per device.

v0:
```python
import math
import jax
import jax.numpy as jnp
from jax import lax
from jax.sharding import PartitionSpec as P

MONARCH = 32
TAPS = 3
EPS = 1e-06
TABLE_PRECISION = lax.Precision.HIGH
FULL_TURN = 2.0 * math.pi


def shifted(block, axis, distance):
    devices = range(lax.axis_size(axis))
    route = [(i - distance, i) for i in devices if i - distance in devices]
    return lax.ppermute(block, axis, route)


def as_sent(value):
    return jax.tree.map(lambda a: a.astype(jnp.bfloat16) if a.dtype == jnp.float32 else a, value)


def turn_table(count, orient):
    index = jnp.arange(count, dtype=jnp.int32)
    angle = FULL_TURN * (index[:, None] * index[None, :] % count).astype(jnp.float32) / count
    return (jnp.cos(angle), orient * jnp.sin(angle))


def twist(real_part, imag_part, table_cos, table_sin, form):
    cos_real = jnp.einsum(form, table_cos, real_part, precision=TABLE_PRECISION)
    sin_real = jnp.einsum(form, table_sin, real_part, precision=TABLE_PRECISION)
    cos_imag = jnp.einsum(form, table_cos, imag_part, precision=TABLE_PRECISION)
    sin_imag = jnp.einsum(form, table_sin, imag_part, precision=TABLE_PRECISION)
    return (cos_real - sin_imag, cos_imag + sin_real)


def local_dft(real_part, imag_part, orient):
    length = real_part.shape[-1]
    first = MONARCH
    second = length // first
    leading = real_part.shape[:-1]
    real_part = real_part.reshape(leading + (first, second))
    imag_part = imag_part.reshape(leading + (first, second))
    cos_first, sin_first = turn_table(first, orient)
    real_part, imag_part = twist(real_part, imag_part, cos_first, sin_first, "ca,...ab->...cb")
    outer_index = jnp.arange(first, dtype=jnp.int32)[:, None]
    inner_index = jnp.arange(second, dtype=jnp.int32)[None, :]
    angle = FULL_TURN * (outer_index * inner_index % length).astype(jnp.float32) / length
    cos_middle = jnp.cos(angle)
    sin_middle = orient * jnp.sin(angle)
    real_part, imag_part = (
        real_part * cos_middle - imag_part * sin_middle,
        imag_part * cos_middle + real_part * sin_middle,
    )
    cos_second, sin_second = turn_table(second, orient)
    real_part, imag_part = twist(real_part, imag_part, cos_second, sin_second, "db,...cb->...dc")
    return (real_part.reshape(leading + (length,)), imag_part.reshape(leading + (length,)))


def rotate(real_part, imag_part, freq_index, row_index, total_length, orient):
    angle = (
        FULL_TURN
        * (freq_index[:, None] * row_index[None, :] % total_length).astype(jnp.float32)
        / total_length
    )
    cos_turn = jnp.cos(angle)[:, None, :]
    sin_turn = orient * jnp.sin(angle)[:, None, :]
    return (
        real_part * cos_turn - imag_part * sin_turn,
        imag_part * cos_turn + real_part * sin_turn,
    )


def block_dft(blocks, row_index, total_length):
    count = blocks.shape[0]
    freq_count = 2 * count
    freq_index = jnp.arange(freq_count, dtype=jnp.int32)
    block_index = jnp.arange(count, dtype=jnp.int32)
    angle = (
        FULL_TURN
        * (freq_index[:, None] * block_index[None, :] % freq_count).astype(jnp.float32)
        / freq_count
    )
    real_part = jnp.einsum("ks,scr->kcr", jnp.cos(angle), blocks, precision=TABLE_PRECISION)
    imag_part = -jnp.einsum("ks,scr->kcr", jnp.sin(angle), blocks, precision=TABLE_PRECISION)
    real_part, imag_part = rotate(real_part, imag_part, freq_index, row_index, total_length, -1.0)
    return jnp.stack([real_part, imag_part])


def block_idft(real_part, imag_part, total_length):
    freq_count = real_part.shape[0]
    count = freq_count // 2
    block_index = jnp.arange(count, dtype=jnp.int32)
    freq_index = jnp.arange(freq_count, dtype=jnp.int32)
    angle = (
        FULL_TURN
        * (block_index[:, None] * freq_index[None, :] % freq_count).astype(jnp.float32)
        / freq_count
    )
    value = jnp.einsum("sk,kcr->scr", jnp.cos(angle), real_part, precision=TABLE_PRECISION)
    value = value - jnp.einsum("sk,kcr->scr", jnp.sin(angle), imag_part, precision=TABLE_PRECISION)
    return value / total_length


def apply_filter(frequency, filter_part):
    real_part, imag_part = local_dft(frequency[0], frequency[1], -1.0)
    filter_real = filter_part[0]
    filter_imag = filter_part[1]
    product_real = real_part * filter_real - imag_part * filter_imag
    product_imag = real_part * filter_imag + imag_part * filter_real
    return local_dft(product_real, product_imag, 1.0)


def per_device(tokens, norm_gain, in_weight, short_filter, filter_spectrum, out_weight):
    seq_count = lax.axis_size("seq")
    seq_place = lax.axis_index("seq")
    inputs = tokens.astype(jnp.float32)
    square_mean = jnp.mean(inputs * inputs, axis=-1, keepdims=True)
    normed = (inputs / jnp.sqrt(square_mean + EPS) * norm_gain).astype(jnp.bfloat16)
    model_width = in_weight.shape[0]
    width = in_weight.shape[2]
    flat_weight = in_weight.reshape(model_width, 3 * width)
    projected = jnp.dot(
        lax.all_gather(normed, "tensor", axis=0, tiled=True),
        flat_weight,
        preferred_element_type=jnp.float32,
    ).astype(jnp.bfloat16)
    rows = projected.shape[0]
    carried = shifted(projected[rows - (TAPS - 1) :], "seq", 1)
    extended = (
        jnp.concatenate([carried, projected], axis=0)
        .astype(jnp.float32)
        .reshape(rows + TAPS - 1, 3, width)
    )
    short = jnp.zeros((rows, 3, width), jnp.float32)
    for offset in range(TAPS):
        short = (
            short + short_filter[offset] * extended[TAPS - 1 - offset : TAPS - 1 - offset + rows]
        )
    queries = short[:, 0]
    product_cols = (short[:, 1] * short[:, 2]).astype(jnp.bfloat16).T
    total_length = 2 * rows * seq_count
    all_rows = jnp.arange(rows, dtype=jnp.int32)
    piece_rows = rows // seq_count
    gathered = lax.all_to_all(
        product_cols.reshape(1, width, rows), "seq", split_axis=2, concat_axis=0, tiled=True
    )
    own_rows = seq_place * piece_rows + jnp.arange(piece_rows, dtype=jnp.int32)
    partial_spec = block_dft(gathered.astype(jnp.float32), own_rows, total_length)
    frequency = lax.all_to_all(
        partial_spec.astype(jnp.bfloat16), "seq", split_axis=1, concat_axis=3, tiled=True
    ).astype(partial_spec.dtype)
    real_part, imag_part = apply_filter(frequency, filter_spectrum)
    own_freq = 2 * seq_place + jnp.arange(2, dtype=jnp.int32)
    real_part, imag_part = rotate(real_part, imag_part, own_freq, all_rows, total_length, 1.0)
    returned = lax.all_to_all(
        jnp.stack([real_part, imag_part]).astype(jnp.bfloat16),
        "seq",
        split_axis=3,
        concat_axis=1,
        tiled=True,
    ).astype(jnp.float32)
    value_blocks = block_idft(returned[0], returned[1], total_length)
    value_cols = lax.all_to_all(
        as_sent(value_blocks), "seq", split_axis=0, concat_axis=2, tiled=True
    ).astype(value_blocks.dtype)
    long_conv = value_cols[0].T
    gated = (queries * long_conv).astype(jnp.bfloat16)
    summed = lax.psum_scatter(
        jnp.dot(gated, out_weight, preferred_element_type=jnp.float32).astype(jnp.bfloat16),
        "tensor",
        scatter_dimension=0,
        tiled=True,
    ).astype(jnp.float32)
    return (inputs + summed).astype(jnp.bfloat16)


def solution(mesh):
    in_specs = (
        P(("seq", "tensor"), None),
        P(),
        P(None, None, "tensor"),
        P(None, None, "tensor"),
        P(None, "seq", "tensor", None),
        P("tensor", None),
    )
    out_specs = P(("seq", "tensor"), None)
    return jax.shard_map(
        per_device, mesh=mesh, in_specs=in_specs, out_specs=out_specs, check_vma=False
    )
```

profile of v0, /device:TPU:0, one launch (start us, length us, event | category | flops | bytes accessed | tf_op | source)
XLA Modules:
  0.0 549.9 jit_solution(9565816952888031319)
XLA Ops:
  6.5 1.5 fusion.36
  8.1 2.5 fusion.38
  10.6 17.1 %copy.89 = bf16[4096,3,512]{0,2,1:T(8,128)(2,1)} copy(bf16[4096,3,512]{2,0,1:T(8,128)(2,1)} %param.8) | data formatting | bytes 25165824 | tf_op args[2]
  27.7 67.8 %all-gather.2.cloned.1.call-done = bf16[1024,4096]{1,0:T(8,128)(2,1)} async-done(((bf16[128,4096]{1,0:T(8,128)(2,1)}), bf16[1024,4096]{1,0:T(8,128)(2,1)}) %all-gather.2.cloned.1.call-update) | async-done | bytes 8388624 | tf_op jit(solution)/shard_map/all_gather | solution.py:125
  95.5 18.3 %convolution_convert_fusion.1 = bf16[1024,1536]{1,0:T(8,128)(2,1)S(1)} fusion(bf16[1024,4096]{1,0:T(8,128)(2,1)} %all-gather.2.cloned.1.call-done, bf16[4096,1536]{0,1:T(8,128)(2,1)} %bitcast.210), kind=kOutput, calls=%fused_computation.50 | convolution fusion | flops 12886474752 | bytes 24117248 | tf_op jit(solution)/shard_map/dot_general | solution.py:124
  113.8 3.4 collective-permute-start
  117.3 1.3 collective-permute-done
  118.6 1.0 maximum_convert_fusion
  119.5 7.4 %fusion.229 = (f32[1024,1536]{1,0:T(8,128)}, f32[1024,1536]{1,0:T(8,128)}, f32[1024,1536]{1,0:T(8,128)}) fusion(f32[1026,1536]{1,0:T(8,128)S(1)} %maximum_convert_fusion), kind=kLoop, calls=%fused_computation.263 | loop fusion | bytes 37748736 | tf_op jit(solution)/shard_map/slice | solution.py:139
  127.0 6.6 %copy.90 = f32[1024,1536]{0,1:T(8,128)} copy(f32[1024,1536]{1,0:T(8,128)} %get-tuple-element.17) | data formatting | bytes 12582912 | tf_op jit(solution)/shard_map/slice | solution.py:139
  133.5 6.6 %copy.91 = f32[1024,1536]{0,1:T(8,128)} copy(f32[1024,1536]{1,0:T(8,128)} %get-tuple-element.19) | data formatting | bytes 12582912 | tf_op jit(solution)/shard_map/slice | solution.py:139
  140.1 6.6 %copy.92 = f32[1024,1536]{0,1:T(8,128)} copy(f32[1024,1536]{1,0:T(8,128)} %get-tuple-element.18) | data formatting | bytes 12582912 | tf_op jit(solution)/shard_map/slice | solution.py:139
  146.7 7.1 %multiply_add_fusion = f32[1024,3,512]{0,2,1:T(8,128)S(1)} fusion(f32[1024,3,512]{0,2,1:T(8,128)} %bitcast.203, f32[1024,3,512]{0,2,1:T(8,128)} %bitcast.202, f32[1024,3,512]{0,2,1:T(8,128)} %bitcast.201, f32[3,512]{1,0:T(4,128)S(1)} %get-tuple-element.25, f32[3,512]{1,0:T(4,128)S(1)} %get-tuple-element.26, f32[3,512]{1,0:T(4,128)S(1)} %get-tuple-element.24), kind=kLoop, calls=%fused_computation.1 | loop fusion | flops 7864320 | bytes 25184256 | tf_op jit(solution)/shard_map/add | solution.py:139
  153.8 2.7 copy-done.1
  157.4 1.6 copy.178
  159.5 7.0 %reduce = bf16[1024,512]{1,0:T(8,128)(2,1)S(1)} reduce(bf16[1024,1,512]{2,1,0:T(2,128)(2,1)S(1)} %bitcast.212, bf16[]{:T(256)} %broadcast.422), dimensions={1}, to_apply=%bitcast.198.reduce_sub_computation | reduce | bytes 2097154
  166.6 2.0 reshape.261
  168.6 4.6 all-to-all-start
  173.3 13.5 %all-to-all-done = bf16[4,2,65536]{2,1,0:T(2,128)(2,1)S(1)} async-done(((bf16[4,2,65536]{2,1,0:T(2,128)(2,1)}), bf16[4,2,65536]{2,1,0:T(2,128)(2,1)S(1)}, u32[]{:S(2)}, u32[]{:S(2)}) %all-to-all-start) | async-done | bytes 1048608 | tf_op jit(solution)/shard_map/all_to_all | solution.py:146
  188.8 1.6 fusion.52
  190.4 3.0 fusion.40
  193.8 2.9 copy.96
  196.7 4.9 all-to-all-start.1
  201.9 8.5 %fusion.228 = (f32[1,2,512,1024]{3,2,1,0:T(8,128)}, f32[1,2,512,1024]{3,2,1,0:T(8,128)}) fusion(f32[2,2,512,1024]{3,2,1,0:T(8,128)} %param.10), kind=kLoop, calls=%fused_computation.262 | loop fusion | bytes 16777216 | tf_op jit(solution)/shard_map/slice | solution.py:108
  210.4 5.4 copy.134
  215.8 5.4 copy.135
  221.6 27.7 %all-to-all-done.1 = bf16[2,8,512,256]{3,2,0,1:T(8,128)(2,1)} async-done(((bf16[2,8,512,256]{3,2,0,1:T(8,128)(2,1)}), bf16[2,8,512,256]{3,2,0,1:T(8,128)(2,1)}, u32[]{:S(2)}, u32[]{:S(2)}) %all-to-all-start.1) | async-done | bytes 4194336 | tf_op jit(solution)/shard_map/all_to_all | solution.py:151
  249.3 2.5 copy.97
  251.8 2.3 fusion.231
  254.0 2.8 copy.98
  256.9 4.3 fusion.49
  261.2 4.5 copy.100
  265.8 4.0 fusion.45
  269.7 2.7 convolution_subtract_fusion.1
  272.4 3.8 fusion.8
  276.3 4.8 fusion.20
  281.1 6.7 %fusion.18 = f32[2,512,32,32]{1,3,2,0:T(8,128)} fusion(f32[2,512,32,32]{1,2,3,0:T(8,128)S(1)} %get-tuple-element.10), kind=kOutput, calls=%fused_computation.42 | convolution fusion | flops 201340928 | bytes 8388608 | tf_op jit(solution)/shard_map/db,...cb->...dc/dot_general | solution.py:33
  287.7 5.1 fusion.26
  292.8 11.7 %fusion.6 = (f32[2,512,32,32]{1,2,3,0:T(8,128)S(1)}, f32[2,512,32,32]{1,2,3,0:T(8,128)S(1)}) fusion(f32[2,512,32,32]{1,3,2,0:T(8,128)S(1)} %fusion.26, f32[2,512,32,32]{1,3,2,0:T(8,128)} %bitcast.207, f32[2,512,32,32]{1,3,2,0:T(8,128)S(1)} %bitcast.206, f32[2,512,32,32]{1,3,2,0:T(8,128)} %fusion.18, f32[2,512,32,32]{1,2,3,0:T(8,128)S(1)} %get-tuple-element.9), kind=kOutput, calls=%fused_computation.20 | convolution fusion | flops 208681984 | bytes 29360128 | tf_op jit(solution)/shard_map/db,...cb->...dc/dot_general | solution.py:32
  304.5 2.4 fusion.72
  306.9 2.4 fusion.70
  309.3 2.7 convolution_subtract_fusion
  312.0 4.0 fusion.4
  316.0 4.8 fusion.12
  320.8 4.7 fusion.10
  325.5 5.1 subtract_bitcast_fusion
  330.6 2.6 copy.119
  333.3 5.1 add_bitcast_fusion
  338.4 2.4 copy.122
  340.8 2.1 fusion.1
  343.3 6.3 %copy.123 = bf16[2,2,512,1024]{2,1,0,3:T(2,128)(2,1)} copy(bf16[2,2,512,1024]{2,3,1,0:T(8,128)(2,1)S(1)} %pad_maximum_fusion.1) | data formatting | bytes 8388608 | tf_op jit(solution)/shard_map/stack | solution.py:158
  349.6 51.2 %all_to_all.57 = bf16[2,2,512,1024]{2,1,0,3:T(2,128)(2,1)S(1)} all-to-all(bf16[2,2,512,1024]{2,1,0,3:T(2,128)(2,1)} %copy.123), channel_id=1, replica_groups=mesh['seq'=4,'tensor'=8] {'seq'}, dimensions={3} | all-to-all | bytes 8388608 | tf_op jit(solution)/shard_map/all_to_all | solution.py:157
  401.6 2.4 fusion.230
  404.0 5.0 copy.125
  409.0 2.2 squeeze.21
  411.2 2.9 fusion.134
  414.1 6.3 %copy.126 = bf16[1,4,2,512,256]{4,2,1,3,0:T(2,128)(2,1)} copy(bf16[1,4,2,512,256]{3,4,1,2,0:T(8,128)(2,1)} %get-tuple-element.20) | data formatting | bytes 4194304 | tf_op jit(solution)/shard_map/slice | solution.py:164
  420.4 4.1 squeeze.22
  424.5 3.2 multiply_convert_fusion
  427.8 14.8 %all_to_all.58 = bf16[4,512,256]{2,1,0:T(8,128)(2,1)S(1)} all-to-all(bf16[4,512,256]{2,1,0:T(8,128)(2,1)S(1)} %copy.127), channel_id=1, replica_groups=mesh['seq'=4,'tensor'=8] {'seq'}, dimensions={0} | all-to-all | bytes 2097152 | tf_op jit(solution)/shard_map/all_to_all | solution.py:165
  442.8 1.4 copy.128
  445.0 8.6 %convolution_convert_fusion = bf16[1024,4096]{1,0:T(8,128)(2,1)} fusion(bf16[512,4096]{1,0:T(8,128)(2,1)S(1)} %copy-done.6, f32[1024,3,512]{0,2,1:T(8,128)} %copy-done.1, f32[512,1024]{1,0:T(8,128)S(1)} %bitcast.216), kind=kOutput, calls=%fused_computation | convolution fusion | flops 4300210176 | bytes 16777216 | tf_op jit(solution)/shard_map/dot_general | solution.py:171
  453.7 86.8 %reduce-scatter.2.cloned.1.call-done = bf16[128,4096]{1,0:T(8,128)(2,1)} async-done(((bf16[1024,4096]{1,0:T(8,128)(2,1)}), bf16[128,4096]{1,0:T(8,128)(2,1)}) %reduce-scatter.2.cloned.1.call-update) | async-done | bytes 1048592 | tf_op jit(solution)/shard_map/reduce_scatter | solution.py:170
  540.4 2.4 fusion.39
  (42 shorter events, 6.9 us)
Async XLA Ops:
  6.5 89.0 %all-gather.2.cloned.1.call-start = ((), (), s32[]{:S(2)}) async-start(), calls=%async_computation.5 | async-start | bytes 9437184 | tf_op jit(solution)/shard_map/all_gather | solution.py:125
  95.5 21.7 %copy-start.5 = (f32[3,3,512]{2,1,0:T(4,128)S(1)}, f32[3,3,512]{2,1,0:T(4,128)}, u32[]{:S(2)}) copy-start(f32[3,3,512]{2,1,0:T(4,128)} %param.9) | copy-start | bytes 55300
  113.8 4.7 collective-permute-start
  153.8 2.7 copy-start.1
  168.6 18.3 %all-to-all-start = ((bf16[4,2,65536]{2,1,0:T(2,128)(2,1)}), bf16[4,2,65536]{2,1,0:T(2,128)(2,1)S(1)}, u32[]{:S(2)}, u32[]{:S(2)}) async-start(bf16[4,2,65536]{2,1,0:T(2,128)(2,1)} %reshape.261), calls=%async_computation | async-start | bytes 2097152 | tf_op jit(solution)/shard_map/all_to_all | solution.py:146
  196.7 52.6 %all-to-all-start.1 = ((bf16[2,8,512,256]{3,2,0,1:T(8,128)(2,1)}), bf16[2,8,512,256]{3,2,0,1:T(8,128)(2,1)}, u32[]{:S(2)}, u32[]{:S(2)}) async-start(bf16[2,8,512,256]{3,2,0,1:T(8,128)(2,1)} %copy.96), calls=%async_computation.1 | async-start | bytes 8388608 | tf_op jit(solution)/shard_map/all_to_all | solution.py:151
  201.5 338.9 %reduce-scatter.2.cloned.1.call-start = ((), (), s32[]{:S(2)}) async-start(), calls=%async_computation.6 | async-start | bytes 9437184 | tf_op jit(solution)/shard_map/reduce_scatter | solution.py:170
  265.7 4.0 copy-start
  265.8 4.0 copy-start.3
  287.7 5.1 copy-start.2
  442.8 2.2 copy-start.6
  453.6 86.8 %copy-start.4 = (bf16[128,4096]{1,0:T(8,128)(2,1)S(1)}, bf16[128,4096]{1,0:T(8,128)(2,1)}, u32[]{:S(2)}) copy-start(bf16[128,4096]{1,0:T(8,128)(2,1)} %param.6) | copy-start | bytes 3145732
Sparse Core Ops, SparseCore 0:
  10.7 84.7 all-gather.1
  453.8 86.5 reduce-scatter.1
where the time goes:
time: 556 us; the launch traced here: 550 us
  waiting for transfers between devices  197 us (35%)
  local copies, waits for them, and re-layouts  123 us (22%)
  matrix products  112 us (20%)
  blocking collectives  65.9 us (12%)
  other arithmetic  25.6 us (5%)
  between operations  14.1 us (3%)
  starting transfers between devices  12.9 us (2%)
    reduce_scatter x1, waiting for transfers between devices, per_device(): lax.psum_scatter(jnp.dot(gated, out_weight, preferred_element_type=jnp.fl...  86.8 us
    all_gather x1, waiting for transfers between devices, per_device(): lax.all_gather(normed, 'tensor', axis=0, tiled=True)  67.8 us
    all_to_all x1, blocking collectives, per_device(): lax.all_to_all(jnp.stack([real_part, imag_part]).astype(jnp.bfloat16), 's...  51.2 us
    unnamed x22, local copies, waits for them, and re-layouts  35.2 us
    all_to_all x1, waiting for transfers between devices, per_device(): lax.all_to_all(partial_spec.astype(jnp.bfloat16), 'seq', split_axis=1, co...  27.7 us
    slice x4, local copies, waits for them, and re-layouts, per_device(): extended[TAPS - 1 - offset:TAPS - 1 - offset + rows]  27.1 us
    dot_general x4, matrix products, twist(): sin_real = jnp.einsum(form, table_sin, real_part, precision=TABLE_PRECISION)  24.6 us
    dot_general x1, matrix products, per_device(): jnp.dot(lax.all_gather(normed, 'tensor', axis=0, tiled=True), flat_weight...  18.3 us
  transfers between devices with their start and end apart: 5, of which 5 were waited for; matrix products, arithmetic and copies ran while one was open for 7% of the time, Pallas kernels for 0%

commit v1 on v0

--- a/solution.py
+++ b/solution.py
@@ -9,6 +9,13 @@
 EPS = 1e-06
 TABLE_PRECISION = lax.Precision.HIGH
 FULL_TURN = 2.0 * math.pi
+
+
+def trade_parts(x, axis, split, join):
+    peers = lax.axis_size(axis)
+    pieces = jnp.stack(jnp.split(x, peers, axis=split), axis=0)
+    pieces = lax.all_to_all(pieces, axis, split_axis=0, concat_axis=0)
+    return jnp.concatenate(pieces, axis=join)
 
 
 def shifted(block, axis, distance):
@@ -154,12 +161,8 @@
     real_part, imag_part = apply_filter(frequency, filter_spectrum)
     own_freq = 2 * seq_place + jnp.arange(2, dtype=jnp.int32)
     real_part, imag_part = rotate(real_part, imag_part, own_freq, all_rows, total_length, 1.0)
-    returned = lax.all_to_all(
-        jnp.stack([real_part, imag_part]).astype(jnp.bfloat16),
-        "seq",
-        split_axis=3,
-        concat_axis=1,
-        tiled=True,
+    returned = trade_parts(
+        jnp.stack([real_part, imag_part]).astype(jnp.bfloat16), "seq", 3, 1
     ).astype(jnp.float32)
     value_blocks = block_idft(returned[0], returned[1], total_length)
     value_cols = lax.all_to_all(

time: 556 us -> 537 us (0.966)
  local copies, waits for them, and re-layouts: 123 us -> 105 us
    slice x3 -> x1, local copies, waits for them, and re-layouts: 13.7 us -> 1.6 us  [per_device(): value_blocks = block_idft(returned[0], returned[1], total_length)]
    another operation x1 -> x0, local copies, waits for them, and re-layouts: 6.26 us -> none  [per_device(): jnp.stack([real_part, imag_part]).astype(jnp.bfloat16)]
where the time goes in v1:
time: 537 us; the launch traced here: 531 us
  waiting for transfers between devices  197 us (37%)
  matrix products  112 us (21%)
  local copies, waits for them, and re-layouts  105 us (20%)
  blocking collectives  64.8 us (12%)
  other arithmetic  25.9 us (5%)
  between operations  14.3 us (3%)
  starting transfers between devices  12.9 us (2%)
    reduce_scatter x1, waiting for transfers between devices, per_device(): lax.psum_scatter(jnp.dot(gated, out_weight, preferred_element_type=jnp.fl...  86.7 us
    all_gather x1, waiting for transfers between devices, per_device(): lax.all_gather(normed, 'tensor', axis=0, tiled=True)  67.8 us
    all_to_all x1, blocking collectives, trade_parts(): pieces = lax.all_to_all(pieces, axis, split_axis=0, concat_axis=0)  50.2 us
    unnamed x22, local copies, waits for them, and re-layouts  35.2 us
    all_to_all x1, waiting for transfers between devices, per_device(): lax.all_to_all(partial_spec.astype(jnp.bfloat16), 'seq', split_axis=1, co...  27.7 us
    slice x4, local copies, waits for them, and re-layouts, per_device(): extended[TAPS - 1 - offset:TAPS - 1 - offset + rows]  27 us
    dot_general x4, matrix products, twist(): sin_real = jnp.einsum(form, table_sin, real_part, precision=TABLE_PRECISION)  24.6 us
    dot_general x1, matrix products, per_device(): jnp.dot(lax.all_gather(normed, 'tensor', axis=0, tiled=True), flat_weight...  18.3 us
  transfers between devices with their start and end apart: 5, of which 5 were waited for; matrix products, arithmetic and copies ran while one was open for 7% of the time, Pallas kernels for 0%

profile of v1, /device:TPU:0, one launch (start us, length us, event | category | flops | bytes accessed | tf_op | source)
XLA Modules:
  0.0 531.4 jit_solution(12565679409207022833)
XLA Ops:
  6.5 1.5 fusion.36
  8.1 2.5 fusion.38
  10.6 17.1 %copy.90 = bf16[4096,3,512]{0,2,1:T(8,128)(2,1)} copy(bf16[4096,3,512]{2,0,1:T(8,128)(2,1)} %param.8) | data formatting | bytes 25165824 | tf_op args[2]
  27.8 67.8 %all-gather.2.cloned.1.call-done = bf16[1024,4096]{1,0:T(8,128)(2,1)} async-done(((bf16[128,4096]{1,0:T(8,128)(2,1)}), bf16[1024,4096]{1,0:T(8,128)(2,1)}) %all-gather.2.cloned.1.call-update) | async-done | bytes 8388624 | tf_op jit(solution)/shard_map/all_gather | solution.py:132
  95.5 18.3 %convolution_convert_fusion.1 = bf16[1024,1536]{1,0:T(8,128)(2,1)S(1)} fusion(bf16[1024,4096]{1,0:T(8,128)(2,1)} %all-gather.2.cloned.1.call-done, bf16[4096,1536]{0,1:T(8,128)(2,1)} %bitcast.214), kind=kOutput, calls=%fused_computation.56 | convolution fusion | flops 12886474752 | bytes 24117248 | tf_op jit(solution)/shard_map/dot_general | solution.py:131
  113.8 3.4 collective-permute-start
  117.3 1.3 collective-permute-done
  118.6 1.0 maximum_convert_fusion
  119.5 7.2 %fusion.236 = (f32[1024,1536]{1,0:T(8,128)}, f32[1024,1536]{1,0:T(8,128)}, f32[1024,1536]{1,0:T(8,128)}) fusion(f32[1026,1536]{1,0:T(8,128)S(1)} %maximum_convert_fusion), kind=kLoop, calls=%fused_computation.277 | loop fusion | bytes 37748736 | tf_op jit(solution)/shard_map/slice | solution.py:146
  126.8 6.6 %copy.91 = f32[1024,1536]{0,1:T(8,128)} copy(f32[1024,1536]{1,0:T(8,128)} %get-tuple-element.17) | data formatting | bytes 12582912 | tf_op jit(solution)/shard_map/slice | solution.py:146
  133.4 6.6 %copy.92 = f32[1024,1536]{0,1:T(8,128)} copy(f32[1024,1536]{1,0:T(8,128)} %get-tuple-element.19) | data formatting | bytes 12582912 | tf_op jit(solution)/shard_map/slice | solution.py:146
  140.0 6.6 %copy.93 = f32[1024,1536]{0,1:T(8,128)} copy(f32[1024,1536]{1,0:T(8,128)} %get-tuple-element.18) | data formatting | bytes 12582912 | tf_op jit(solution)/shard_map/slice | solution.py:146
  146.6 7.1 %multiply_add_fusion = f32[1024,3,512]{0,2,1:T(8,128)S(1)} fusion(f32[1024,3,512]{0,2,1:T(8,128)} %bitcast.207, f32[1024,3,512]{0,2,1:T(8,128)} %bitcast.206, f32[1024,3,512]{0,2,1:T(8,128)} %bitcast.205, f32[3,512]{1,0:T(4,128)S(1)} %get-tuple-element.29, f32[3,512]{1,0:T(4,128)S(1)} %get-tuple-element.30, f32[3,512]{1,0:T(4,128)S(1)} %get-tuple-element.28), kind=kLoop, calls=%fused_computation.1 | loop fusion | flops 7864320 | bytes 25184256 | tf_op jit(solution)/shard_map/add | solution.py:146
  153.7 2.7 copy-done.1
  157.3 1.6 copy.179
  159.4 7.0 %reduce = bf16[1024,512]{1,0:T(8,128)(2,1)S(1)} reduce(bf16[1024,1,512]{2,1,0:T(2,128)(2,1)S(1)} %bitcast.216, bf16[]{:T(256)} %broadcast.422), dimensions={1}, to_apply=%bitcast.202.reduce_sub_computation | reduce | bytes 2097154
  166.5 2.0 reshape.266
  168.5 4.6 all-to-all-start
  173.2 13.5 %all-to-all-done = bf16[4,2,65536]{2,1,0:T(2,128)(2,1)S(1)} async-done(((bf16[4,2,65536]{2,1,0:T(2,128)(2,1)}), bf16[4,2,65536]{2,1,0:T(2,128)(2,1)S(1)}, u32[]{:S(2)}, u32[]{:S(2)}) %all-to-all-start) | async-done | bytes 1048608 | tf_op jit(solution)/shard_map/all_to_all | solution.py:153
  186.7 0.9 reshape.267
  188.0 0.7 copy.131
  188.7 1.6 fusion.59
  190.3 3.0 fusion.40
  193.7 2.9 copy.97
  196.6 4.9 all-to-all-start.1
  201.8 8.6 %fusion.235 = (f32[1,2,512,1024]{3,2,1,0:T(8,128)}, f32[1,2,512,1024]{3,2,1,0:T(8,128)}) fusion(f32[2,2,512,1024]{3,2,1,0:T(8,128)} %param.10), kind=kLoop, calls=%fused_computation.276 | loop fusion | bytes 16777216 | tf_op jit(solution)/shard_map/slice | solution.py:115
  210.4 5.4 %copy.135 = f32[1,2,512,1024]{2,3,1,0:T(8,128)} copy(f32[1,2,512,1024]{3,2,1,0:T(8,128)} %get-tuple-element.15) | data formatting | bytes 8388608
  215.7 5.4 %copy.136 = f32[1,2,512,1024]{2,3,1,0:T(8,128)} copy(f32[1,2,512,1024]{3,2,1,0:T(8,128)} %get-tuple-element.16) | data formatting | bytes 8388608
  221.5 27.7 %all-to-all-done.1 = bf16[2,8,512,256]{3,2,0,1:T(8,128)(2,1)} async-done(((bf16[2,8,512,256]{3,2,0,1:T(8,128)(2,1)}), bf16[2,8,512,256]{3,2,0,1:T(8,128)(2,1)}, u32[]{:S(2)}, u32[]{:S(2)}) %all-to-all-start.1) | async-done | bytes 4194336 | tf_op jit(solution)/shard_map/all_to_all | solution.py:158
  249.2 2.5 copy.98
  251.6 2.3 fusion.238
  253.9 2.8 copy.99
  256.7 4.3 fusion.49
  261.1 4.5 copy.101
  265.7 3.9 fusion.45
  269.6 2.7 convolution_subtract_fusion.1
  272.3 3.8 fusion.8
  276.2 4.8 fusion.20
  281.0 6.6 %fusion.18 = f32[2,512,32,32]{1,3,2,0:T(8,128)} fusion(f32[2,512,32,32]{1,2,3,0:T(8,128)S(1)} %get-tuple-element.10), kind=kOutput, calls=%fused_computation.48 | convolution fusion | flops 201340928 | bytes 8388608 | tf_op jit(solution)/shard_map/db,...cb->...dc/dot_general | solution.py:40
  287.6 5.1 fusion.26
  292.7 11.7 %fusion.6 = (f32[2,512,32,32]{1,2,3,0:T(8,128)S(1)}, f32[2,512,32,32]{1,2,3,0:T(8,128)S(1)}) fusion(f32[2,512,32,32]{1,3,2,0:T(8,128)S(1)} %fusion.26, f32[2,512,32,32]{1,3,2,0:T(8,128)} %bitcast.211, f32[2,512,32,32]{1,3,2,0:T(8,128)S(1)} %bitcast.210, f32[2,512,32,32]{1,3,2,0:T(8,128)} %fusion.18, f32[2,512,32,32]{1,2,3,0:T(8,128)S(1)} %get-tuple-element.9), kind=kOutput, calls=%fused_computation.26 | convolution fusion | flops 208681984 | bytes 29360128 | tf_op jit(solution)/shard_map/db,...cb->...dc/dot_general | solution.py:39
  304.4 2.4 fusion.79
  306.8 2.4 fusion.77
  309.2 2.7 convolution_subtract_fusion
  311.9 4.0 fusion.4
  315.9 4.8 fusion.12
  320.7 4.7 fusion.10
  325.4 5.1 subtract_bitcast_fusion
  330.5 2.6 copy.120
  333.2 5.1 add_bitcast_fusion
  338.3 2.4 copy.123
  340.7 1.7 fusion.1
  343.0 0.6 pad_maximum_fusion.1
  343.5 50.2 %all_to_all.47 = bf16[4,2,2,512,256]{3,4,2,1,0:T(8,128)(2,1)S(1)} all-to-all(bf16[4,2,2,512,256]{3,4,2,1,0:T(8,128)(2,1)S(1)} %pad_maximum_fusion.1), channel_id=1, replica_groups=mesh['seq'=4,'tensor'=8] {'seq'}, dimensions={0} | all-to-all | bytes 8388608 | tf_op jit(solution)/shard_map/all_to_all | solution.py:17
  393.7 1.6 fusion.237
  395.3 3.1 copy.132
  398.4 2.9 fusion.141
  401.3 4.5 copy.133
  405.8 3.1 multiply_convert_fusion
  409.1 14.6 %all_to_all.48 = bf16[4,512,256]{2,1,0:T(8,128)(2,1)S(1)} all-to-all(bf16[4,512,256]{2,1,0:T(8,128)(2,1)S(1)} %copy.126), channel_id=1, replica_groups=mesh['seq'=4,'tensor'=8] {'seq'}, dimensions={0} | all-to-all | bytes 2097152 | tf_op jit(solution)/shard_map/all_to_all | solution.py:168
  423.9 1.4 copy.127
  426.1 8.8 %convolution_convert_fusion = bf16[1024,4096]{1,0:T(8,128)(2,1)} fusion(bf16[512,4096]{1,0:T(8,128)(2,1)S(1)} %copy-done.6, f32[1024,3,512]{0,2,1:T(8,128)} %copy-done.1, f32[512,1024]{1,0:T(8,128)S(1)} %bitcast.222), kind=kOutput, calls=%fused_computation | convolution fusion | flops 4300210176 | bytes 16777216 | tf_op jit(solution)/shard_map/dot_general | solution.py:174
  434.9 86.7 %reduce-scatter.2.cloned.1.call-done = bf16[128,4096]{1,0:T(8,128)(2,1)} async-done(((bf16[1024,4096]{1,0:T(8,128)(2,1)}), bf16[128,4096]{1,0:T(8,128)(2,1)}) %reduce-scatter.2.cloned.1.call-update) | async-done | bytes 1048592 | tf_op jit(solution)/shard_map/reduce_scatter | solution.py:173
  521.6 2.4 fusion.39
  (39 shorter events, 4.6 us)
Async XLA Ops:
  6.5 89.0 %all-gather.2.cloned.1.call-start = ((), (), s32[]{:S(2)}) async-start(), calls=%async_computation.5 | async-start | bytes 9437184 | tf_op jit(solution)/shard_map/all_gather | solution.py:132
  95.5 21.7 %copy-start.5 = (f32[3,3,512]{2,1,0:T(4,128)S(1)}, f32[3,3,512]{2,1,0:T(4,128)}, u32[]{:S(2)}) copy-start(f32[3,3,512]{2,1,0:T(4,128)} %param.9) | copy-start | bytes 55300
  113.8 4.8 collective-permute-start
  153.7 2.7 copy-start.1
  168.5 18.3 %all-to-all-start = ((bf16[4,2,65536]{2,1,0:T(2,128)(2,1)}), bf16[4,2,65536]{2,1,0:T(2,128)(2,1)S(1)}, u32[]{:S(2)}, u32[]{:S(2)}) async-start(bf16[4,2,65536]{2,1,0:T(2,128)(2,1)} %reshape.266), calls=%async_computation | async-start | bytes 2097152 | tf_op jit(solution)/shard_map/all_to_all | solution.py:153
  196.6 52.6 %all-to-all-start.1 = ((bf16[2,8,512,256]{3,2,0,1:T(8,128)(2,1)}), bf16[2,8,512,256]{3,2,0,1:T(8,128)(2,1)}, u32[]{:S(2)}, u32[]{:S(2)}) async-start(bf16[2,8,512,256]{3,2,0,1:T(8,128)(2,1)} %copy.97), calls=%async_computation.1 | async-start | bytes 8388608 | tf_op jit(solution)/shard_map/all_to_all | solution.py:158
  201.4 320.2 %reduce-scatter.2.cloned.1.call-start = ((), (), s32[]{:S(2)}) async-start(), calls=%async_computation.6 | async-start | bytes 9437184 | tf_op jit(solution)/shard_map/reduce_scatter | solution.py:173
  265.6 4.0 copy-start
  265.6 4.0 copy-start.3
  287.6 5.1 copy-start.2
  423.9 2.2 copy-start.6
  434.9 86.8 %copy-start.4 = (bf16[128,4096]{1,0:T(8,128)(2,1)S(1)}, bf16[128,4096]{1,0:T(8,128)(2,1)}, u32[]{:S(2)}) copy-start(bf16[128,4096]{1,0:T(8,128)(2,1)} %param.6) | copy-start | bytes 3145732
Sparse Core Ops, SparseCore 0:
  10.7 84.7 all-gather.1
  435.0 86.5 reduce-scatter.1
